TPU v7x, 256 devices: a whole 4x4x8 slice. The times are simulated.
256 devices in a mesh: users: 16 (over x_hi, z), seq: 16 (over x_lo, y, core).
Axes of the slice: x: 4 (x_hi: 2, x_lo: 2; x = x_hi * 2 + x_lo), y: 4, z: 8, core: 2. Of those that a mesh axis runs over, the one named last changes fastest.
Arguments:
- hist_qu: bfloat16 [16, 2048, 2, 512], P('users', 'seq'), may hold values from -6 to 6
- hist_kv: bfloat16 [16, 2048, 2, 512], P('users', 'seq'), may hold values from -6 to 6
- hist_x: bfloat16 [16, 2048, 1024], P('users', 'seq'), may hold values from -6 to 6
- lengths: int32 [16], P('users'), may hold values from 512 to 2048, as said below
- cand_qu: bfloat16 [16, 16, 384, 2, 512], P('users', 'seq'), may hold values from -6 to 6
- cand_owner: int32 [16, 16, 12], P('users', 'seq'), may hold values from 0 to 15, as said below
- w_out: bfloat16 [512, 1024], replicated, may hold values from -0.25 to 0.25
Outputs:
- hist_out: bfloat16 [16, 2048, 1024], P('users', 'seq')
- cand_out: bfloat16 [16, 16, 384, 1024], P('users', 'seq')
Inputs may be any that keep to these rules, and one draw needn't show every extreme that they name: `lengths`: some user has exactly 2048 events. `cand_owner`: one device names one owner at most 2 times; for every index of seq some owner is named exactly 2 times by each device of that index.
All inputs are finite; a program needn't handle non-finite values.
Results may differ from a plain program's by a relative error of at most 0.0064.
Values may be sent and summed in bfloat16 or wider, within the bound.
A program may use at most 64 MiB of HBM per device.

v0:
```python
import math

import jax
import jax.numpy as jnp
from jax import lax
from jax.sharding import PartitionSpec as P

HEADS = 4
HEAD_DIM = 128
CAP = 2


EPS = 1e-05


def apply_gate_values(normed, gates):
    return (normed.astype(jnp.float32) * gates.astype(jnp.float32)).astype(jnp.bfloat16)


def local(hist_qu, hist_kv, hist_x, lengths, cand_qu, cand_owner, w_out):
    users = lax.axis_size("users")
    seqs = lax.axis_size("seq")
    mine = lax.axis_index("seq")
    rows = hist_qu.shape[1]
    width = hist_qu.shape[3]
    limit = lengths[0]
    owners = cand_owner[0, 0]
    tiles = owners.shape[0]
    tile = cand_qu.shape[2] // tiles
    slots = CAP
    same = owners[:, None] == owners[None, :]
    before = jnp.arange(tiles)[None, :] < jnp.arange(tiles)[:, None]
    ranks = jnp.sum(same & before, axis=1)
    target = owners * slots + ranks
    placement_plan = (
        jnp.arange(users * slots, dtype=jnp.int32)[:, None] == target[None, :]
    ).astype(jnp.bfloat16)
    arrived = users * slots * tile
    rows_per_tile = cand_qu[0, 0].reshape(tiles, tile, 2 * width)
    outgoing = jnp.einsum(
        "yq,qbi->ybi", placement_plan, rows_per_tile, preferred_element_type=jnp.float32
    ).astype(jnp.bfloat16)
    incoming = lax.all_to_all(
        outgoing.reshape(users, slots * tile, 2 * width),
        "users",
        split_axis=0,
        concat_axis=0,
        tiled=True,
    )
    incoming = incoming.reshape(arrived, 2, width)
    arrived_queries = incoming[:, 0]
    arrived_gates = incoming[:, 1]
    total = rows + arrived
    queries = jnp.concatenate([hist_qu[0, :, 0], arrived_queries], axis=0).reshape(
        total, HEADS, HEAD_DIM
    )
    first_row = mine * rows
    qpos = jnp.concatenate(
        [
            first_row + jnp.arange(rows, dtype=jnp.int32),
            jnp.full((arrived,), rows * seqs, jnp.int32),
        ]
    )
    scale = 1.0 / math.sqrt(HEAD_DIM)

    def attend(summed, part, first):
        count = part.shape[0]
        kpos = first + jnp.arange(count, dtype=jnp.int32)
        keys = part[:, 0].reshape(count, HEADS, HEAD_DIM)
        value_rows = part[:, 1].reshape(count, HEADS, HEAD_DIM)
        scores = (
            jnp.einsum("qhd,khd->hqk", queries, keys, preferred_element_type=jnp.float32) * scale
        )
        allowed = (kpos[None, :] < limit) & (kpos[None, :] <= qpos[:, None])
        weights = jnp.where(allowed[None], jax.nn.silu(scores), 0.0).astype(jnp.bfloat16)
        update = jnp.einsum("hqk,khd->qhd", weights, value_rows, preferred_element_type=jnp.float32)
        return summed + update.reshape(total, width)

    def visit(summed, part, first):
        return attend(summed, part, first)

    piece = lax.all_gather(hist_kv[0], "seq", axis=0, tiled=True)
    count = piece.shape[0]
    step = math.gcd(count, 128)

    def one_step(index, carry):
        part = lax.dynamic_slice_in_dim(piece, index * step, step, 0)
        return visit(carry, part, index * step)

    summed = lax.fori_loop(0, count // step, one_step, jnp.zeros((total, width), jnp.float32))
    mean = jnp.mean(summed, axis=-1, keepdims=True)
    centred = summed - mean
    spread = jnp.mean(centred * centred, axis=-1, keepdims=True)
    normed = (centred * lax.rsqrt(spread + EPS)).astype(jnp.bfloat16)
    hist_gated = apply_gate_values(normed[:rows], hist_qu[0, :, 1])
    hist_rows = jnp.dot(hist_gated, w_out, preferred_element_type=jnp.float32) + hist_x[0].astype(
        jnp.float32
    )
    inside = first_row + jnp.arange(rows, dtype=jnp.int32) < limit
    hist_out = jnp.where(inside[:, None], hist_rows, 0.0).astype(jnp.bfloat16)[None]
    model_width = w_out.shape[1]
    cand_gated = apply_gate_values(normed[rows:], arrived_gates)
    projected = jnp.dot(cand_gated, w_out, preferred_element_type=jnp.float32).astype(jnp.bfloat16)
    returned = lax.all_to_all(
        projected.reshape(users, slots * tile, model_width),
        "users",
        split_axis=0,
        concat_axis=0,
        tiled=True,
    )
    picked = jnp.einsum(
        "st,srx->trx",
        placement_plan,
        returned.reshape(users * slots, tile, model_width),
        preferred_element_type=jnp.float32,
    )
    cand_rows = picked.astype(jnp.bfloat16).reshape(tiles * tile, model_width)
    return (hist_out, cand_rows.reshape(1, 1, tiles * tile, model_width))


def solution(mesh):
    placed = (
        P("users", "seq", None, None),
        P("users", "seq", None, None),
        P("users", "seq", None),
        P("users"),
        P("users", "seq", None, None, None),
        P("users", "seq", None),
        P(),
    )
    return jax.shard_map(
        local,
        mesh=mesh,
        in_specs=placed,
        out_specs=(P("users", "seq", None), P("users", "seq", None, None)),
        check_vma=False,
    )
```

profile of v0, /device:TPU:32, one launch (start us, length us, event | category | flops | bytes accessed | tf_op | source)
XLA Modules:
  0.0 331.4 jit_solution(1112374799685719295)
XLA Ops:
  17.1 11.0 %all-to-all-start = ((bf16[16,64,1024]{2,1,0:T(8,128)(2,1)}), bf16[16,64,1024]{2,1,0:T(8,128)(2,1)}, u32[]{:S(2)}, u32[]{:S(2)}) async-start(bf16[16,64,1024]{2,1,0:T(8,128)(2,1)} %bitcast.5), calls=%async_computation | async-start | bytes 4194304 | tf_op jit(solution)/shard_map/all_to_all | solution.py:43
  32.1 46.5 %all-to-all-done = bf16[16,64,1024]{2,1,0:T(8,128)(2,1)} async-done(((bf16[16,64,1024]{2,1,0:T(8,128)(2,1)}), bf16[16,64,1024]{2,1,0:T(8,128)(2,1)}, u32[]{:S(2)}, u32[]{:S(2)}) %all-to-all-start) | async-done | bytes 2097184 | tf_op jit(solution)/shard_map/all_to_all | solution.py:43
  78.6 4.5 %reshape.115 = bf16[1024,2,512]{2,1,0:T(2,128)(2,1)} reshape(bf16[16,64,1024]{2,1,0:T(8,128)(2,1)} %all-to-all-done) | data formatting | bytes 4194304 | tf_op jit(solution)/shard_map/reshape | solution.py:50
  83.1 6.8 %slice_convert_fusion = (f32[1024,1,512]{2,1,0:T(1,128)}, bf16[1024,1,512]{2,1,0:T(2,128)(2,1)}) fusion(bf16[1024,2,512]{2,1,0:T(2,128)(2,1)} %reshape.115), kind=kLoop, calls=%fused_computation.19 | loop fusion | flops 524288 | bytes 5242880 | tf_op jit(solution)/shard_map/convert_element_type | solution.py:17
  89.9 5.8 %copy.44 = bf16[1024,1,512]{0,2,1:T(8,128)(2,1)} copy(bf16[1024,1,512]{2,1,0:T(2,128)(2,1)} %get-tuple-element.160) | data formatting | bytes 2097152 | tf_op jit(solution)/shard_map/slice | solution.py:51
  100.6 154.9 %while.14 = (s32[]{:T(128)}, f32[1152,512]{0,1:T(8,128)S(1)}, bf16[2048,2,512]{0,2,1:T(8,128)(2,1)}, s32[]{:T(128)}, s32[1152]{0:T(1024)}, /*index=5*/bf16[1152,...) while((s32[]{:T(128)}, f32[1152,512]{0,1:T(8,128)S(1)}, ...), condition=%wide.region_2.3_spmd.clone, body=%wide.region_1.2_spmd.clone.sunk | while | flops 307593600 | bytes 11704269 | solution.py:90
  103.8 4.2 %fusion.43 = f32[4,128,1152]{2,1,0:T(8,128)} fusion(bf16[128,4,128]{0,2,1:T(8,128)(2,1)} %bitcast.65, bf16[128,4,128]{0,2,1:T(8,128)(2,1)} %bitcast.64, bf16[1152,4,128]{2,0,1:T(8,128)(2,1)} %get-tuple-element.231, pred[1152,128]{0,1:T(8,128)(4,1)S(1)} %compare_and_fusion.2), kind=kOutput, calls=%fused_computation.4.clone.1 | convolution fusion | flops 306118656 | bytes 3948544 | tf_op jit(solution)/shard_map/while/body/eval_jaxpr/hqk,khd->qhd/dot_general | solution.py:76
  113.5 4.2 %fusion.43 = f32[4,128,1152]{2,1,0:T(8,128)} fusion(bf16[128,4,128]{0,2,1:T(8,128)(2,1)} %bitcast.65, bf16[128,4,128]{0,2,1:T(8,128)(2,1)} %bitcast.64, bf16[1152,4,128]{2,0,1:T(8,128)(2,1)} %get-tuple-element.231, pred[1152,128]{0,1:T(8,128)(4,1)S(1)} %compare_and_fusion.2), kind=kOutput, calls=%fused_computation.4.clone.1 | convolution fusion | flops 306118656 | bytes 3948544 | tf_op jit(solution)/shard_map/while/body/eval_jaxpr/hqk,khd->qhd/dot_general | solution.py:76
  123.2 4.2 %fusion.43 = f32[4,128,1152]{2,1,0:T(8,128)} fusion(bf16[128,4,128]{0,2,1:T(8,128)(2,1)} %bitcast.65, bf16[128,4,128]{0,2,1:T(8,128)(2,1)} %bitcast.64, bf16[1152,4,128]{2,0,1:T(8,128)(2,1)} %get-tuple-element.231, pred[1152,128]{0,1:T(8,128)(4,1)S(1)} %compare_and_fusion.2), kind=kOutput, calls=%fused_computation.4.clone.1 | convolution fusion | flops 306118656 | bytes 3948544 | tf_op jit(solution)/shard_map/while/body/eval_jaxpr/hqk,khd->qhd/dot_general | solution.py:76
  132.9 4.2 %fusion.43 = f32[4,128,1152]{2,1,0:T(8,128)} fusion(bf16[128,4,128]{0,2,1:T(8,128)(2,1)} %bitcast.65, bf16[128,4,128]{0,2,1:T(8,128)(2,1)} %bitcast.64, bf16[1152,4,128]{2,0,1:T(8,128)(2,1)} %get-tuple-element.231, pred[1152,128]{0,1:T(8,128)(4,1)S(1)} %compare_and_fusion.2), kind=kOutput, calls=%fused_computation.4.clone.1 | convolution fusion | flops 306118656 | bytes 3948544 | tf_op jit(solution)/shard_map/while/body/eval_jaxpr/hqk,khd->qhd/dot_general | solution.py:76
  142.6 4.2 %fusion.43 = f32[4,128,1152]{2,1,0:T(8,128)} fusion(bf16[128,4,128]{0,2,1:T(8,128)(2,1)} %bitcast.65, bf16[128,4,128]{0,2,1:T(8,128)(2,1)} %bitcast.64, bf16[1152,4,128]{2,0,1:T(8,128)(2,1)} %get-tuple-element.231, pred[1152,128]{0,1:T(8,128)(4,1)S(1)} %compare_and_fusion.2), kind=kOutput, calls=%fused_computation.4.clone.1 | convolution fusion | flops 306118656 | bytes 3948544 | tf_op jit(solution)/shard_map/while/body/eval_jaxpr/hqk,khd->qhd/dot_general | solution.py:76
  152.2 4.2 %fusion.43 = f32[4,128,1152]{2,1,0:T(8,128)} fusion(bf16[128,4,128]{0,2,1:T(8,128)(2,1)} %bitcast.65, bf16[128,4,128]{0,2,1:T(8,128)(2,1)} %bitcast.64, bf16[1152,4,128]{2,0,1:T(8,128)(2,1)} %get-tuple-element.231, pred[1152,128]{0,1:T(8,128)(4,1)S(1)} %compare_and_fusion.2), kind=kOutput, calls=%fused_computation.4.clone.1 | convolution fusion | flops 306118656 | bytes 3948544 | tf_op jit(solution)/shard_map/while/body/eval_jaxpr/hqk,khd->qhd/dot_general | solution.py:76
  161.9 4.2 %fusion.43 = f32[4,128,1152]{2,1,0:T(8,128)} fusion(bf16[128,4,128]{0,2,1:T(8,128)(2,1)} %bitcast.65, bf16[128,4,128]{0,2,1:T(8,128)(2,1)} %bitcast.64, bf16[1152,4,128]{2,0,1:T(8,128)(2,1)} %get-tuple-element.231, pred[1152,128]{0,1:T(8,128)(4,1)S(1)} %compare_and_fusion.2), kind=kOutput, calls=%fused_computation.4.clone.1 | convolution fusion | flops 306118656 | bytes 3948544 | tf_op jit(solution)/shard_map/while/body/eval_jaxpr/hqk,khd->qhd/dot_general | solution.py:76
  171.6 4.2 %fusion.43 = f32[4,128,1152]{2,1,0:T(8,128)} fusion(bf16[128,4,128]{0,2,1:T(8,128)(2,1)} %bitcast.65, bf16[128,4,128]{0,2,1:T(8,128)(2,1)} %bitcast.64, bf16[1152,4,128]{2,0,1:T(8,128)(2,1)} %get-tuple-element.231, pred[1152,128]{0,1:T(8,128)(4,1)S(1)} %compare_and_fusion.2), kind=kOutput, calls=%fused_computation.4.clone.1 | convolution fusion | flops 306118656 | bytes 3948544 | tf_op jit(solution)/shard_map/while/body/eval_jaxpr/hqk,khd->qhd/dot_general | solution.py:76
  181.3 4.2 %fusion.43 = f32[4,128,1152]{2,1,0:T(8,128)} fusion(bf16[128,4,128]{0,2,1:T(8,128)(2,1)} %bitcast.65, bf16[128,4,128]{0,2,1:T(8,128)(2,1)} %bitcast.64, bf16[1152,4,128]{2,0,1:T(8,128)(2,1)} %get-tuple-element.231, pred[1152,128]{0,1:T(8,128)(4,1)S(1)} %compare_and_fusion.2), kind=kOutput, calls=%fused_computation.4.clone.1 | convolution fusion | flops 306118656 | bytes 3948544 | tf_op jit(solution)/shard_map/while/body/eval_jaxpr/hqk,khd->qhd/dot_general | solution.py:76
  190.9 4.2 %fusion.43 = f32[4,128,1152]{2,1,0:T(8,128)} fusion(bf16[128,4,128]{0,2,1:T(8,128)(2,1)} %bitcast.65, bf16[128,4,128]{0,2,1:T(8,128)(2,1)} %bitcast.64, bf16[1152,4,128]{2,0,1:T(8,128)(2,1)} %get-tuple-element.231, pred[1152,128]{0,1:T(8,128)(4,1)S(1)} %compare_and_fusion.2), kind=kOutput, calls=%fused_computation.4.clone.1 | convolution fusion | flops 306118656 | bytes 3948544 | tf_op jit(solution)/shard_map/while/body/eval_jaxpr/hqk,khd->qhd/dot_general | solution.py:76
  200.6 4.2 %fusion.43 = f32[4,128,1152]{2,1,0:T(8,128)} fusion(bf16[128,4,128]{0,2,1:T(8,128)(2,1)} %bitcast.65, bf16[128,4,128]{0,2,1:T(8,128)(2,1)} %bitcast.64, bf16[1152,4,128]{2,0,1:T(8,128)(2,1)} %get-tuple-element.231, pred[1152,128]{0,1:T(8,128)(4,1)S(1)} %compare_and_fusion.2), kind=kOutput, calls=%fused_computation.4.clone.1 | convolution fusion | flops 306118656 | bytes 3948544 | tf_op jit(solution)/shard_map/while/body/eval_jaxpr/hqk,khd->qhd/dot_general | solution.py:76
  210.3 4.2 %fusion.43 = f32[4,128,1152]{2,1,0:T(8,128)} fusion(bf16[128,4,128]{0,2,1:T(8,128)(2,1)} %bitcast.65, bf16[128,4,128]{0,2,1:T(8,128)(2,1)} %bitcast.64, bf16[1152,4,128]{2,0,1:T(8,128)(2,1)} %get-tuple-element.231, pred[1152,128]{0,1:T(8,128)(4,1)S(1)} %compare_and_fusion.2), kind=kOutput, calls=%fused_computation.4.clone.1 | convolution fusion | flops 306118656 | bytes 3948544 | tf_op jit(solution)/shard_map/while/body/eval_jaxpr/hqk,khd->qhd/dot_general | solution.py:76
  220.0 4.2 %fusion.43 = f32[4,128,1152]{2,1,0:T(8,128)} fusion(bf16[128,4,128]{0,2,1:T(8,128)(2,1)} %bitcast.65, bf16[128,4,128]{0,2,1:T(8,128)(2,1)} %bitcast.64, bf16[1152,4,128]{2,0,1:T(8,128)(2,1)} %get-tuple-element.231, pred[1152,128]{0,1:T(8,128)(4,1)S(1)} %compare_and_fusion.2), kind=kOutput, calls=%fused_computation.4.clone.1 | convolution fusion | flops 306118656 | bytes 3948544 | tf_op jit(solution)/shard_map/while/body/eval_jaxpr/hqk,khd->qhd/dot_general | solution.py:76
  229.7 4.2 %fusion.43 = f32[4,128,1152]{2,1,0:T(8,128)} fusion(bf16[128,4,128]{0,2,1:T(8,128)(2,1)} %bitcast.65, bf16[128,4,128]{0,2,1:T(8,128)(2,1)} %bitcast.64, bf16[1152,4,128]{2,0,1:T(8,128)(2,1)} %get-tuple-element.231, pred[1152,128]{0,1:T(8,128)(4,1)S(1)} %compare_and_fusion.2), kind=kOutput, calls=%fused_computation.4.clone.1 | convolution fusion | flops 306118656 | bytes 3948544 | tf_op jit(solution)/shard_map/while/body/eval_jaxpr/hqk,khd->qhd/dot_general | solution.py:76
  239.3 4.2 %fusion.43 = f32[4,128,1152]{2,1,0:T(8,128)} fusion(bf16[128,4,128]{0,2,1:T(8,128)(2,1)} %bitcast.65, bf16[128,4,128]{0,2,1:T(8,128)(2,1)} %bitcast.64, bf16[1152,4,128]{2,0,1:T(8,128)(2,1)} %get-tuple-element.231, pred[1152,128]{0,1:T(8,128)(4,1)S(1)} %compare_and_fusion.2), kind=kOutput, calls=%fused_computation.4.clone.1 | convolution fusion | flops 306118656 | bytes 3948544 | tf_op jit(solution)/shard_map/while/body/eval_jaxpr/hqk,khd->qhd/dot_general | solution.py:76
  249.0 4.2 %fusion.43 = f32[4,128,1152]{2,1,0:T(8,128)} fusion(bf16[128,4,128]{0,2,1:T(8,128)(2,1)} %bitcast.65, bf16[128,4,128]{0,2,1:T(8,128)(2,1)} %bitcast.64, bf16[1152,4,128]{2,0,1:T(8,128)(2,1)} %get-tuple-element.231, pred[1152,128]{0,1:T(8,128)(4,1)S(1)} %compare_and_fusion.2), kind=kOutput, calls=%fused_computation.4.clone.1 | convolution fusion | flops 306118656 | bytes 3948544 | tf_op jit(solution)/shard_map/while/body/eval_jaxpr/hqk,khd->qhd/dot_general | solution.py:76
  264.4 6.0 %all-to-all-start.1 = ((bf16[16,64,1024]{2,1,0:T(8,128)(2,1)}), bf16[16,64,1024]{2,1,0:T(8,128)(2,1)S(1)}, u32[]{:S(2)}, u32[]{:S(2)}) async-start(bf16[16,64,1024]{2,1,0:T(8,128)(2,1)} %bitcast.10), calls=%async_computation.1 | async-start | bytes 4194304 | tf_op jit(solution)/shard_map/all_to_all | solution.py:104
  273.1 47.8 %all-to-all-done.1 = bf16[16,64,1024]{2,1,0:T(8,128)(2,1)S(1)} async-done(((bf16[16,64,1024]{2,1,0:T(8,128)(2,1)}), bf16[16,64,1024]{2,1,0:T(8,128)(2,1)S(1)}, u32[]{:S(2)}, u32[]{:S(2)}) %all-to-all-start.1) | async-done | bytes 2097184 | tf_op jit(solution)/shard_map/all_to_all | solution.py:104
  (123 shorter events, 120.9 us)
Async XLA Ops:
  7.2 253.3 %copy-start = (bf16[512,1024]{1,0:T(8,128)(2,1)S(1)}, bf16[512,1024]{1,0:T(8,128)(2,1)}, u32[]{:S(2)}) copy-start(bf16[512,1024]{1,0:T(8,128)(2,1)} %param.15) | copy-start | bytes 3145732
  7.2 5.2 %copy-start.7 = (s32[1,1,12]{2,1,0:T(1,128)S(1)}, s32[1,1,12]{2,1,0:T(1,128)}, u32[]{:S(2)}) copy-start(s32[1,1,12]{2,1,0:T(1,128)} %param.14) | copy-start | bytes 148
  7.2 93.4 %all-gather.3.cloned.1.call-start = ((), (), s32[]{:S(2)}) async-start(), calls=%async_computation.2 | async-start | bytes 4456448 | tf_op jit(solution)/shard_map/all_gather | solution.py:82
  12.6 4.5 %copy-start.5 = (s32[12]{0:T(128)}, s32[12]{0:T(128)S(1)}, u32[]{:S(2)}) copy-start(s32[12]{0:T(128)S(1)} %multiply_add_fusion) | copy-start | bytes 148
  17.1 61.5 %all-to-all-start = ((bf16[16,64,1024]{2,1,0:T(8,128)(2,1)}), bf16[16,64,1024]{2,1,0:T(8,128)(2,1)}, u32[]{:S(2)}, u32[]{:S(2)}) async-start(bf16[16,64,1024]{2,1,0:T(8,128)(2,1)} %bitcast.5), calls=%async_computation | async-start | bytes 4194304 | tf_op jit(solution)/shard_map/all_to_all | solution.py:43
  257.7 2.4 copy-start.1
  259.9 1.9 copy-start.2
  260.4 4.0 %copy-start.3 = (bf16[1152,512]{1,0:T(8,128)(2,1)}, bf16[1152,512]{1,0:T(8,128)(2,1)S(1)}, u32[]{:S(2)}) copy-start(bf16[1152,512]{1,0:T(8,128)(2,1)S(1)} %multiply_convert_fusion) | copy-start | bytes 3538948
  264.4 6.6 %copy-start.4 = (bf16[1,128,1,512]{3,2,1,0:T(2,128)(2,1)S(1)}, bf16[1,128,1,512]{3,2,1,0:T(2,128)(2,1)}, u32[]{:S(2)}) copy-start(bf16[1,128,1,512]{3,2,1,0:T(2,128)(2,1)} %get-tuple-element.161) | copy-start | bytes 393220
  264.4 56.5 %copy-start.6 = (s32[12]{0:T(128)S(1)}, s32[12]{0:T(128)}, u32[]{:S(2)}) copy-start(s32[12]{0:T(128)} %copy-done.5) | copy-start | bytes 148
  264.4 56.5 %all-to-all-start.1 = ((bf16[16,64,1024]{2,1,0:T(8,128)(2,1)}), bf16[16,64,1024]{2,1,0:T(8,128)(2,1)S(1)}, u32[]{:S(2)}, u32[]{:S(2)}) async-start(bf16[16,64,1024]{2,1,0:T(8,128)(2,1)} %bitcast.10), calls=%async_computation.1 | async-start | bytes 4194304 | tf_op jit(solution)/shard_map/all_to_all | solution.py:104
Sparse Core Ops, SparseCore 0:
  10.4 60.4 all-gather.2
where the time goes:
time: 334 us; the launch traced here: 331 us
  waiting for transfers between devices  94.3 us (28%)
  matrix products  75.3 us (23%)
  other arithmetic  72.9 us (22%)
  local copies, waits for them, and re-layouts  56.2 us (17%)
  starting transfers between devices  17 us (5%)
  between operations  14.8 us (4%)
    dot_general x16, matrix products, attend(): jnp.einsum('hqk,khd->qhd', weights, value_rows, preferred_element_type=jn...  66.5 us
    all_to_all x1, waiting for transfers between devices, local(): lax.all_to_all(projected.reshape(users, slots * tile, model_width), 'user...  47.8 us
    all_to_all x1, waiting for transfers between devices, local(): lax.all_to_all(outgoing.reshape(users, slots * tile, 2 * width), 'users',...  46.5 us
    add x16, other arithmetic, attend(): return summed + update.reshape(total, width)  36.3 us
    slice x16, local copies, waits for them, and re-layouts, attend(): keys = part[:, 0].reshape(count, HEADS, HEAD_DIM)  27 us
    and x16, other arithmetic, attend(): allowed = (kpos[None, :] < limit) & (kpos[None, :] <= qpos[:, None])  13.8 us
    all_to_all x1, starting transfers between devices, local(): lax.all_to_all(outgoing.reshape(users, slots * tile, 2 * width), 'users',...  11 us
    lt x16, other arithmetic, attend(): allowed = (kpos[None, :] < limit) & (kpos[None, :] <= qpos[:, None])  10.4 us
  transfers between devices with their start and end apart: 3, of which 2 were waited for; matrix products, arithmetic and copies ran while one was open for 11% of the time, Pallas kernels for 0%

commit v1 on v0

v1 whole, which is shorter than its diff:
```python
import functools
import math

import jax
import jax.numpy as jnp
from jax import lax
from jax.experimental import pallas as pl
from jax.experimental.pallas import tpu as pltpu
from jax.sharding import PartitionSpec as P

HEADS = 4
HEAD_DIM = 128
WIDTH = HEADS * HEAD_DIM
CAP = 2
TILE = 32
TILES = 12
CROWS = TILES * TILE
ROWS = 128
LENGTH = 2048
MODEL = 1024
EPS = 1e-05
HALF_SCALE = 0.5 / math.sqrt(HEAD_DIM)

ZS, YS = 8, 4
HOPS = 4
MESSAGES = HOPS * 4
PACK = CAP * TILE
BATCH = 512
BATCHES = MESSAGES * PACK // BATCH
PER_BATCH = MESSAGES // BATCHES


def _mod(value, size):
    return lax.rem(value + 2 * size, size)


def _user(x_hi, z):
    return _mod(x_hi, 2) * ZS + _mod(z, ZS)


def _seq(x_lo, y, core):
    return _mod(x_lo, 2) * (YS * 2) + _mod(y, YS) * 2 + _mod(core, 2)


def _send(src, dst, send_sem, recv_sem, device):
    return pltpu.make_async_remote_copy(
        src_ref=src,
        dst_ref=dst,
        send_sem=send_sem,
        recv_sem=recv_sem,
        device_id=device,
        device_id_type=pl.DeviceIdType.MESH,
    )


def _silu_weights(scores):
    half = scores * HALF_SCALE
    return half + half * jnp.tanh(half)


def _normalise(summed):
    mean = jnp.mean(summed, axis=-1, keepdims=True)
    centred = summed - mean
    spread = jnp.mean(centred * centred, axis=-1, keepdims=True)
    return (centred * lax.rsqrt(spread + EPS)).astype(jnp.bfloat16)


def _every_second(rows, first):
    count = rows.shape[0] // 2
    at = 2 * lax.broadcasted_iota(jnp.int32, (count, 2 * count), 0) + first
    column = lax.broadcasted_iota(jnp.int32, (count, 2 * count), 1)
    return jnp.dot(
        jnp.where(column == at, 1.0, 0.0).astype(jnp.bfloat16),
        rows,
        preferred_element_type=jnp.float32,
    ).astype(jnp.bfloat16)


def _gate(normed, gates):
    return (normed.astype(jnp.float32) * gates.astype(jnp.float32)).astype(jnp.bfloat16)


def kernel(
    qu_ref, kv_ref, x_ref, lengths_ref, cand_ref, owner_ref, w_ref,
    hist_out, cand_out,
    own_kv, kv, hist_q, hist_part, hist_done, cand_rows, cand_g, hist_g, outgoing, arrived, computed,
    returned, acc, pick,
    kv_send, kv_recv, q_send, q_recv, r_send, r_recv, h_send, h_recv,
):
    user = lax.axis_index("users")
    seq = lax.axis_index("seq")
    x_hi, z = user // ZS, user % ZS
    x_lo, y, core = seq // (YS * 2), (seq // 2) % YS, seq % 2
    home_x = z // 4
    native = x_lo == home_x

    far = jnp.where(core == 0, 2, -2)
    steps = (0, 1, far, -1)

    def peer(m, back):
        step, a, b = steps[m // 4], (m // 2) % 2, m % 2
        other_z = z + step if back else z - step
        return (_user(x_hi + a, other_z), _seq(x_lo + b, y, core))

    partner = (user, _seq(x_lo, y, core + 1))
    y_up = (user, _seq(x_lo, y + 1, core))
    y_down = (user, _seq(x_lo, y - 1, core))
    x_other = (user, _seq(x_lo + 1, y, core))
    opposite = _user(x_hi, z + 4)

    barrier = pltpu.get_barrier_semaphore()
    greeted = [partner, y_up, y_down]
    greeted += [(opposite, _seq(x_lo, y, core)), (opposite, _seq(x_lo + 1, y, core))]
    greeted += [peer(m, False) for m in range(1, MESSAGES)]
    greeted += [peer(m, True) for m in range(8, 12)]
    for device in greeted:
        pl.semaphore_signal(
            barrier, inc=1, device_id=device, device_id_type=pl.DeviceIdType.MESH
        )

    limit = lengths_ref[0]
    position = seq * ROWS + lax.broadcasted_iota(jnp.int32, (ROWS, WIDTH), 0)
    rows_kv = kv_ref[0].reshape(2 * ROWS, WIDTH)
    own_kv[0] = _every_second(rows_kv, 0)
    own_kv[1] = jnp.where(position < limit, _every_second(rows_kv, 1), jnp.zeros((), jnp.bfloat16))
    hist_q[0] = _every_second(qu_ref[0].reshape(2 * ROWS, WIDTH), 0)

    pl.semaphore_wait(barrier, len(greeted))

    def shard(index):
        return kv.at[:, pl.ds(pl.multiple_of(index * ROWS, ROWS), ROWS), :]

    to_far = _send(
        own_kv, shard(seq), kv_send.at[0], kv_recv.at[seq], (opposite, _seq(home_x, y, core))
    )
    to_near = _send(own_kv, shard(seq), kv_send.at[1], kv_recv.at[seq], x_other)
    q_over = _send(hist_q.at[0], hist_q.at[1], h_send.at[0], h_recv.at[0], x_other)
    to_far.start()

    @pl.when(jnp.logical_not(native))
    def _():
        to_near.start()
        q_over.start()

    @pl.when(native)
    def _():
        kv[:, pl.ds(pl.multiple_of(seq * ROWS, ROWS), ROWS), :] = own_kv[...]

    owners = [owner_ref[0, 0, t] for t in range(TILES)]

    def slot_rows(index):
        tile = index // TILE
        owner = jnp.zeros_like(index)
        for t in range(TILES):
            owner = jnp.where(tile == t, owners[t], owner)
        again = jnp.zeros_like(index)
        for t in range(TILES - 1):
            again = jnp.where((tile > t) & (owner == owners[t]), 1, again)
        owner_x, owner_z = owner >> 3, owner & 7
        a, b = (owner_x + x_hi) & 1, ((owner_z >> 2) + x_lo) & 1
        message = ((z + 8 - owner_z) & 3) * 4 + a * 2 + b
        return message * PACK + again * TILE + (index & (TILE - 1))

    for t in range(TILES * TILE // ROWS):
        cand_rows[pl.ds(t * 2 * ROWS, 2 * ROWS), :] = cand_ref[
            0, 0, t * ROWS : (t + 1) * ROWS
        ].reshape(2 * ROWS, WIDTH)
    column = lax.broadcasted_iota(jnp.int32, (8, 2 * CROWS), 1)
    slot = jnp.where((column & 1) == 0, slot_rows(column >> 1), -1)[:1]
    q_copies = [None] * MESSAGES
    for step in (2, 1, 3, 0):
        block = pl.ds(step * 4 * PACK, 4 * PACK)
        row = step * 4 * PACK + lax.broadcasted_iota(jnp.int32, (4 * PACK, 2 * CROWS), 0)
        outgoing[block, :] = jnp.dot(
            jnp.where(row == slot, 1.0, 0.0).astype(jnp.bfloat16),
            cand_rows[...],
            preferred_element_type=jnp.float32,
        ).astype(jnp.bfloat16)
        for m in range(step * 4, step * 4 + 4):
            part = pl.ds(m * PACK, PACK)
            if m:
                q_copies[m] = _send(
                    outgoing.at[part], arrived.at[part], q_send.at[m], q_recv.at[m], peer(m, False)
                )
                q_copies[m].start()
            else:
                arrived[part, :] = outgoing[part, :]

    kv_copies = []

    def forward(index, device):
        copy = _send(
            shard(index), shard(index), kv_send.at[2 + len(kv_copies)], kv_recv.at[index], device
        )
        copy.start()
        kv_copies.append(copy)

    def await_shard(index):
        _send(shard(index), shard(index), kv_send.at[0], kv_recv.at[index], partner).wait_recv()

    for side in range(2):
        index = _seq(side, y, core)

        @pl.when(jnp.logical_not(jnp.logical_and(native, x_lo == side)))
        def _():
            await_shard(index)

        forward(index, y_up)
        forward(index, y_down)
        forward(index, partner)

    for t in range(TILES * TILE // ROWS):
        cand_g[pl.ds(t * ROWS, ROWS), :] = _every_second(
            cand_rows[pl.ds(t * 2 * ROWS, 2 * ROWS), :], 1
        )
    hist_g[...] = _every_second(qu_ref[0].reshape(2 * ROWS, WIDTH), 1)
    for t in range(TILES * TILE // ROWS):
        held = slot_rows(t * ROWS + lax.broadcasted_iota(jnp.int32, (ROWS, 128), 0))
        at = lax.broadcasted_iota(jnp.int32, (ROWS, MESSAGES * PACK), 1)
        pick[pl.ds(t * ROWS, ROWS), :] = jnp.where(at == held[:, :1], 1.0, 0.0).astype(jnp.bfloat16)

    for side, dy, onward in (
        (0, -1, y_up), (1, 1, y_down), (1, -1, None), (0, 1, None), (0, 2, None), (1, 2, None),
    ):
        index = _seq(side, y + dy, core)
        await_shard(index)
        if onward is not None:
            forward(index, onward)
        forward(index, partner)
    for side in range(2):
        for dy in range(YS):
            await_shard(_seq(side, y + dy, core + 1))

    def attend(queries, count, allowed=None):
        for h in range(HEADS):
            part = slice(h * HEAD_DIM, (h + 1) * HEAD_DIM)
            scores = lax.dot_general(
                queries[:, part],
                kv[0, :, part],
                (((1,), (1,)), ((), ())),
                preferred_element_type=jnp.float32,
            )
            weights = _silu_weights(scores)
            if allowed is not None:
                weights = jnp.where(allowed, weights, 0.0)
            acc[pl.ds(0, count), part] = jnp.dot(
                weights.astype(jnp.bfloat16),
                kv[1, :, part],
                preferred_element_type=jnp.float32,
            )
        return _normalise(acc[pl.ds(0, count), :])

    back_over = _send(hist_part, hist_done, h_send.at[1], h_recv.at[1], x_other)

    @pl.when(native)
    def _():
        q_over.wait_recv()
        key_at = lax.broadcasted_iota(jnp.int32, (ROWS, LENGTH), 1)
        row_at = lax.broadcasted_iota(jnp.int32, (ROWS, LENGTH), 0)
        other = _seq(x_lo + 1, y, core)
        hist_part[...] = attend(hist_q[1], ROWS, key_at <= row_at + other * ROWS)
        back_over.start()
        hist_done[...] = attend(hist_q[0], ROWS, key_at <= row_at + seq * ROWS)

    r_copies = []
    for batch in range(BATCHES):
        for m in range(batch * PER_BATCH, (batch + 1) * PER_BATCH):
            if m:
                q_copies[m].wait_recv()
        part = pl.ds(batch * BATCH, BATCH)
        computed[part, :] = attend(arrived[part, :], BATCH)
        for m in range(batch * PER_BATCH, (batch + 1) * PER_BATCH):
            part = pl.ds(m * PACK, PACK)
            if m:
                copy = _send(
                    computed.at[part], returned.at[part], r_send.at[m], r_recv.at[m], peer(m, True)
                )
                copy.start()
                r_copies.append(copy)
            else:
                returned[part, :] = computed[part, :]

    @pl.when(jnp.logical_not(native))
    def _():
        back_over.wait_recv()

    hist_rows = jnp.dot(
        _gate(hist_done[...], hist_g[...]), w_ref[...], preferred_element_type=jnp.float32
    ) + x_ref[0].astype(jnp.float32)
    row = seq * ROWS + lax.broadcasted_iota(jnp.int32, (ROWS, MODEL), 0)
    hist_out[0] = jnp.where(row < limit, hist_rows, 0.0).astype(jnp.bfloat16)

    for copy in r_copies:
        copy.wait_recv()
    picked = jnp.dot(pick[...], returned[...], preferred_element_type=jnp.float32)
    cand_out[0, 0] = jnp.dot(
        _gate(picked, cand_g[...]), w_ref[...], preferred_element_type=jnp.float32
    ).astype(jnp.bfloat16)

    to_far.wait_send()

    @pl.when(jnp.logical_not(native))
    def _():
        to_near.wait_send()
        q_over.wait_send()

    @pl.when(native)
    def _():
        back_over.wait_send()

    for copy in kv_copies + q_copies[1:] + r_copies:
        copy.wait_send()


def local(hist_qu, hist_kv, hist_x, lengths, cand_qu, cand_owner, w_out):
    vmem = pl.BlockSpec(memory_space=pltpu.VMEM)
    smem = pl.BlockSpec(memory_space=pltpu.SMEM)
    bf16 = jnp.bfloat16
    return pl.pallas_call(
        kernel,
        out_shape=(
            jax.ShapeDtypeStruct((1, ROWS, MODEL), bf16),
            jax.ShapeDtypeStruct((1, 1, CROWS, MODEL), bf16),
        ),
        in_specs=[vmem, vmem, vmem, smem, vmem, smem, vmem],
        out_specs=(vmem, vmem),
        scratch_shapes=[
            pltpu.VMEM((2, ROWS, WIDTH), bf16),
            pltpu.VMEM((2, LENGTH, WIDTH), bf16),
            pltpu.VMEM((2, ROWS, WIDTH), bf16),
            pltpu.VMEM((ROWS, WIDTH), bf16),
            pltpu.VMEM((ROWS, WIDTH), bf16),
            pltpu.VMEM((2 * CROWS, WIDTH), bf16),
            pltpu.VMEM((CROWS, WIDTH), bf16),
            pltpu.VMEM((ROWS, WIDTH), bf16),
            pltpu.VMEM((MESSAGES * PACK, WIDTH), bf16),
            pltpu.VMEM((MESSAGES * PACK, WIDTH), bf16),
            pltpu.VMEM((MESSAGES * PACK, WIDTH), bf16),
            pltpu.VMEM((MESSAGES * PACK, WIDTH), bf16),
            pltpu.VMEM((BATCH, WIDTH), jnp.float32),
            pltpu.VMEM((CROWS, MESSAGES * PACK), bf16),
            pltpu.SemaphoreType.DMA((16,)),
            pltpu.SemaphoreType.DMA((16,)),
            pltpu.SemaphoreType.DMA((MESSAGES,)),
            pltpu.SemaphoreType.DMA((MESSAGES,)),
            pltpu.SemaphoreType.DMA((MESSAGES,)),
            pltpu.SemaphoreType.DMA((MESSAGES,)),
            pltpu.SemaphoreType.DMA((2,)),
            pltpu.SemaphoreType.DMA((2,)),
        ],
        compiler_params=pltpu.CompilerParams(
            collective_id=0, has_side_effects=True, vmem_limit_bytes=50 * 2**20
        ),
    )(hist_qu, hist_kv, hist_x, lengths, cand_qu, cand_owner, w_out)


def solution(mesh):
    placed = (
        P("users", "seq", None, None),
        P("users", "seq", None, None),
        P("users", "seq", None),
        P("users"),
        P("users", "seq", None, None, None),
        P("users", "seq", None),
        P(),
    )
    return jax.shard_map(
        local,
        mesh=mesh,
        in_specs=placed,
        out_specs=(P("users", "seq", None), P("users", "seq", None, None)),
        check_vma=False,
    )
```

time: 334 us -> 80.1 us (0.24)
  the two profiles are of different devices: /device:TPU:32 before, /device:TPU:1 now
where the time goes in v1:
time: 80.1 us; the launch traced here: 79.8 us
  Pallas kernels  71.7 us (90%)
  local copies, waits for them, and re-layouts  6.79 us (8%)
  between operations  1.33 us (2%)
    pallas_call x1, Pallas kernels, local(): pl.pallas_call(kernel, out_shape=(jax.ShapeDtypeStruct((1, ROWS, MODEL),...  71.7 us
    unnamed x14, local copies, waits for them, and re-layouts  6.79 us

profile of v1, /device:TPU:1, one launch (start us, length us, event | category | flops | bytes accessed | tf_op | source)
XLA Modules:
  0.0 79.8 jit_solution(12411959840650975195)
XLA Ops:
  0.6 0.0 copy-start.5
  1.3 0.0 copy-done.5
  1.3 0.0 copy-start
  1.3 1.2 %copy-done = bf16[512,1024]{1,0:T(8,128)(2,1)S(1)} copy-done((bf16[512,1024]{1,0:T(8,128)(2,1)S(1)}, bf16[512,1024]{1,0:T(8,128)(2,1)}, u32[]{:S(2)}) %copy-start) | copy-done | bytes 1048600
  2.5 0.0 copy-start.1
  2.5 1.1 %copy-done.1 = bf16[1,1,384,2,512]{4,3,2,1,0:T(2,128)(2,1)S(1)} copy-done((bf16[1,1,384,2,512]{4,3,2,1,0:T(2,128)(2,1)S(1)}, bf16[1,1,384,2,512]{4,3,2,1,0:T(2,128)(2,1)}, u32[]{:S(2)}) %copy-start.1) | copy-done | bytes 786456
  3.7 0.0 copy-start.2
  3.7 0.9 %copy-done.2 = bf16[1,128,2,512]{3,2,1,0:T(2,128)(2,1)S(1)} copy-done((bf16[1,128,2,512]{3,2,1,0:T(2,128)(2,1)S(1)}, bf16[1,128,2,512]{3,2,1,0:T(2,128)(2,1)}, u32[]{:S(2)}) %copy-start.2) | copy-done | bytes 262168
  4.6 0.0 copy-start.3
  4.6 0.9 %copy-done.3 = bf16[1,128,2,512]{3,2,1,0:T(2,128)(2,1)S(1)} copy-done((bf16[1,128,2,512]{3,2,1,0:T(2,128)(2,1)S(1)}, bf16[1,128,2,512]{3,2,1,0:T(2,128)(2,1)}, u32[]{:S(2)}) %copy-start.3) | copy-done | bytes 262168
  5.6 0.0 copy-start.4
  5.6 0.9 %copy-done.4 = bf16[1,128,1024]{2,1,0:T(8,128)(2,1)S(1)} copy-done((bf16[1,128,1024]{2,1,0:T(8,128)(2,1)S(1)}, bf16[1,128,1024]{2,1,0:T(8,128)(2,1)}, u32[]{:S(2)}) %copy-start.4) | copy-done | bytes 262168
  6.5 71.7 %shard_map.86 = (bf16[1,128,1024]{2,1,0:T(8,128)(2,1)S(1)}, bf16[1,1,384,1024]{3,2,1,0:T(8,128)(2,1)S(1)}) custom-call(bf16[1,128,2,512]{3,2,1,0:T(2,128)(2,1)S(1)} %copy-done.2, bf16[1,128,2,512]{3,2,1,0:T(2,128)(2,1)S(1)} %copy-done.3, bf16[1,128,1024]{2,1,0:T(8,128)(2,1)S(1)} %copy-done.4, s32[1]{0:T(128)S(6)} %copy.11.lengths_ref, ...), custom_call_target="tpu_custom_call" | custom-call | tf_op jit(solution)/shard_map/pallas_call | solution.py:319
  78.2 0.7 copy.12
  78.9 0.9 %copy.13 = bf16[1,1,384,1024]{3,2,1,0:T(8,128)(2,1)} copy(bf16[1,1,384,1024]{3,2,1,0:T(8,128)(2,1)S(1)} %get-tuple-element.5) | data formatting | bytes 1572864
Async XLA Ops:
  0.6 0.7 copy-start.5
  1.3 1.2 %copy-start = (bf16[512,1024]{1,0:T(8,128)(2,1)S(1)}, bf16[512,1024]{1,0:T(8,128)(2,1)}, u32[]{:S(2)}) copy-start(bf16[512,1024]{1,0:T(8,128)(2,1)} %w_ref.1) | copy-start | bytes 3145732
  2.5 1.1 %copy-start.1 = (bf16[1,1,384,2,512]{4,3,2,1,0:T(2,128)(2,1)S(1)}, bf16[1,1,384,2,512]{4,3,2,1,0:T(2,128)(2,1)}, u32[]{:S(2)}) copy-start(bf16[1,1,384,2,512]{4,3,2,1,0:T(2,128)(2,1)} %cand_ref.1) | copy-start | bytes 2359300
  3.7 0.9 %copy-start.2 = (bf16[1,128,2,512]{3,2,1,0:T(2,128)(2,1)S(1)}, bf16[1,128,2,512]{3,2,1,0:T(2,128)(2,1)}, u32[]{:S(2)}) copy-start(bf16[1,128,2,512]{3,2,1,0:T(2,128)(2,1)} %qu_ref.1) | copy-start | bytes 786436
  4.6 0.9 %copy-start.3 = (bf16[1,128,2,512]{3,2,1,0:T(2,128)(2,1)S(1)}, bf16[1,128,2,512]{3,2,1,0:T(2,128)(2,1)}, u32[]{:S(2)}) copy-start(bf16[1,128,2,512]{3,2,1,0:T(2,128)(2,1)} %kv_ref.1) | copy-start | bytes 786436
  5.6 0.9 %copy-start.4 = (bf16[1,128,1024]{2,1,0:T(8,128)(2,1)S(1)}, bf16[1,128,1024]{2,1,0:T(8,128)(2,1)}, u32[]{:S(2)}) copy-start(bf16[1,128,1024]{2,1,0:T(8,128)(2,1)} %x_ref.1) | copy-start | bytes 786436

commit v2 on v1

v2 whole, which is shorter than its diff:
```python
import functools
import math

import jax
import jax.numpy as jnp
from jax import lax
from jax.experimental import pallas as pl
from jax.experimental.pallas import tpu as pltpu
from jax.sharding import PartitionSpec as P

HEADS = 4
HEAD_DIM = 128
WIDTH = HEADS * HEAD_DIM
CAP = 2
TILE = 32
TILES = 12
CROWS = TILES * TILE
ROWS = 128
LENGTH = 2048
MODEL = 1024
EPS = 1e-05
HALF_SCALE = 0.5 / math.sqrt(HEAD_DIM)

ZS, YS = 8, 4
STEPS = 4
MESSAGES = STEPS * 4
Q_ORDER = (12, 13, 14, 15, 4, 8, 5, 9, 6, 10, 7, 11, 1, 2, 3)
PACK = CAP * TILE
PACKED = MESSAGES * PACK
GROUPS = ((0, 8), (8, 8))
QUERY_HEADS = 1
BACK_HEADS = 1


def _mod(value, size):
    return lax.rem(value + 2 * size, size)


def _user(x_hi, z):
    return _mod(x_hi, 2) * ZS + _mod(z, ZS)


def _seq(x_lo, y, core):
    return _mod(x_lo, 2) * (YS * 2) + _mod(y, YS) * 2 + _mod(core, 2)


def _send(src, dst, send_sem, recv_sem, device):
    return pltpu.make_async_remote_copy(
        src_ref=src,
        dst_ref=dst,
        send_sem=send_sem,
        recv_sem=recv_sem,
        device_id=device,
        device_id_type=pl.DeviceIdType.MESH,
    )


def _silu_weights(scores):
    half = scores * HALF_SCALE
    return half + half * jnp.tanh(half)


def _normalise(summed):
    mean = jnp.mean(summed, axis=-1, keepdims=True)
    centred = summed - mean
    spread = jnp.mean(centred * centred, axis=-1, keepdims=True)
    return (centred * lax.rsqrt(spread + EPS)).astype(jnp.bfloat16)


def _every_second(rows, first):
    count = rows.shape[0] // 2
    at = 2 * lax.broadcasted_iota(jnp.int32, (count, 2 * count), 0) + first
    column = lax.broadcasted_iota(jnp.int32, (count, 2 * count), 1)
    return jnp.dot(
        jnp.where(column == at, 1.0, 0.0).astype(jnp.bfloat16),
        rows,
        preferred_element_type=jnp.float32,
    ).astype(jnp.bfloat16)


def _gate(normed, gates):
    return (normed.astype(jnp.float32) * gates.astype(jnp.float32)).astype(jnp.bfloat16)


def kernel(
    qu_hbm, kv_hbm, x_hbm, lengths_hbm, cand_hbm, owner_hbm, w_hbm,
    hist_out, cand_out,
    qu_ref, kv_ref, x_ref, lengths_ref, cand_ref, owner_ref, w_ref,
    own_kv, kv, hist_q, hist_done, cand_rows, cand_g, hist_g, outgoing, arrived, computed,
    returned, pick,
    loaded, kv_send, kv_recv, q_send, q_recv, r_send, r_recv, h_send, h_recv,
):
    user = lax.axis_index("users")
    seq = lax.axis_index("seq")
    x_hi, z = user // ZS, user % ZS
    x_lo, y, core = seq // (YS * 2), (seq // 2) % YS, seq % 2
    home_x = z % 2
    native = x_lo == home_x
    up = 1 - 2 * home_x
    steps = (0, 1, -1, 2)

    def peer(m, back):
        step, a, b = steps[m // 4], (m // 2) % 2, m % 2
        along = -2 if back and step == 2 else step
        return (_user(x_hi + a, z + up * along), _seq(x_lo + b, y, core))

    partner = (user, _seq(x_lo, y, core + 1))
    y_up = (user, _seq(x_lo, y + 1, core))
    y_down = (user, _seq(x_lo, y - 1, core))
    x_other = (user, _seq(x_lo + 1, y, core))
    mate = _user(x_hi, z + 3 * up)

    barrier = pltpu.get_barrier_semaphore()
    greeted = [partner, y_up, y_down]
    greeted += [(mate, _seq(x_lo, y, core)), (mate, _seq(x_lo + 1, y, core))]
    greeted += [peer(m, False) for m in range(1, MESSAGES)]
    greeted += [peer(m, True) for m in range(12, 16)]
    for device in greeted:
        pl.semaphore_signal(
            barrier, inc=1, device_id=device, device_id_type=pl.DeviceIdType.MESH
        )

    pairs = (
        (kv_hbm, kv_ref), (lengths_hbm, lengths_ref), (qu_hbm, qu_ref), (cand_hbm, cand_ref),
        (owner_hbm, owner_ref), (w_hbm, w_ref), (x_hbm, x_ref),
    )
    loads = [pltpu.make_async_copy(a, b, loaded.at[i]) for i, (a, b) in enumerate(pairs)]
    for load in loads:
        load.start()

    loads[0].wait()
    loads[1].wait()
    limit = lengths_ref[0]
    position = seq * ROWS + lax.broadcasted_iota(jnp.int32, (ROWS, WIDTH), 0)
    rows_kv = kv_ref[0].reshape(2 * ROWS, WIDTH)
    keys = _every_second(rows_kv, 0)
    values = jnp.where(position < limit, _every_second(rows_kv, 1), jnp.zeros((), jnp.bfloat16))
    for h in range(HEADS):
        part = slice(h * HEAD_DIM, (h + 1) * HEAD_DIM)
        own_kv[h, 0] = keys[:, part]
        own_kv[h, 1] = values[:, part]
    loads[2].wait()
    hist_q[:ROWS, :] = _every_second(qu_ref[0].reshape(2 * ROWS, WIDTH), 0)

    pl.semaphore_wait(barrier, len(greeted))

    def shard(h, index):
        return kv.at[h, :, pl.ds(pl.multiple_of(index * ROWS, ROWS), ROWS), :]

    home = _seq(home_x, y, core)
    to_far = [
        _send(
            own_kv.at[h], shard(h, seq), kv_send.at[h], kv_recv.at[seq, h], (mate, home)
        )
        for h in range(HEADS)
    ]
    to_near = [
        _send(own_kv.at[h], shard(h, seq), kv_send.at[4 + h], kv_recv.at[seq, h], x_other)
        for h in range(HEADS)
    ]
    q_over = _send(
        hist_q.at[pl.ds(0, ROWS)], hist_q.at[pl.ds(ROWS, ROWS)], h_send.at[0], h_recv.at[0], x_other
    )
    for copy in to_far:
        copy.start()

    @pl.when(jnp.logical_not(native))
    def _():
        for copy in to_near:
            copy.start()
        q_over.start()

    @pl.when(native)
    def _():
        kv[:, :, pl.ds(pl.multiple_of(seq * ROWS, ROWS), ROWS), :] = own_kv[...]

    loads[3].wait()
    loads[4].wait()
    owners = [owner_ref[0, 0, t] for t in range(TILES)]

    def slot_rows(index):
        tile = index // TILE
        owner = jnp.zeros_like(index)
        for t in range(TILES):
            owner = jnp.where(tile == t, owners[t], owner)
        again = jnp.zeros_like(index)
        for t in range(TILES - 1):
            again = jnp.where((tile > t) & (owner == owners[t]), 1, again)
        owner_x, owner_z = owner >> 3, owner & 7
        a, b = (owner_x + x_hi) & 1, (owner_z + x_lo) & 1
        apart = (up * (owner_z - z)) & 7
        step = jnp.zeros_like(index)
        for there in ((1, 6), (4, 7), (2, 5)):
            here = (apart == there[0]) | (apart == there[1])
            step = jnp.where(here, 1 + ((1, 6), (4, 7), (2, 5)).index(there), step)
        message = step * 4 + a * 2 + b
        return message * PACK + again * TILE + (index & (TILE - 1))

    for t in range(TILES * TILE // ROWS):
        cand_rows[pl.ds(t * 2 * ROWS, 2 * ROWS), :] = cand_ref[
            0, 0, t * ROWS : (t + 1) * ROWS
        ].reshape(2 * ROWS, WIDTH)
    column = lax.broadcasted_iota(jnp.int32, (8, 2 * CROWS), 1)
    slot = jnp.where((column & 1) == 0, slot_rows(column >> 1), -1)[:1]
    for step in range(STEPS):
        block = pl.ds(step * 4 * PACK, 4 * PACK)
        row = step * 4 * PACK + lax.broadcasted_iota(jnp.int32, (4 * PACK, 2 * CROWS), 0)
        outgoing[block, :] = jnp.dot(
            jnp.where(row == slot, 1.0, 0.0).astype(jnp.bfloat16),
            cand_rows[...],
            preferred_element_type=jnp.float32,
        ).astype(jnp.bfloat16)
    own_rows = pl.ds(0, PACK)
    arrived[own_rows, :] = outgoing[own_rows, :]

    def columns(first, count):
        return pl.ds(first * HEAD_DIM, count * HEAD_DIM)

    q_copies = {}
    for h in range(0, HEADS, QUERY_HEADS):
        for m in Q_ORDER:
            part = (pl.ds(m * PACK, PACK), columns(h, QUERY_HEADS))
            q_copies[m, h] = _send(
                outgoing.at[part], arrived.at[part], q_send.at[m, h], q_recv.at[m, h], peer(m, False)
            )
            q_copies[m, h].start()

    kv_copies = []

    def forward(h, index, device):
        copy = _send(
            shard(h, index),
            shard(h, index),
            kv_send.at[8 + len(kv_copies)],
            kv_recv.at[index, h],
            device,
        )
        copy.start()
        kv_copies.append(copy)

    def await_shard(h, index):
        _send(
            shard(h, index), shard(h, index), kv_send.at[0], kv_recv.at[index, h], partner
        ).wait_recv()

    def enter(h):
        for side in range(2):
            index = _seq(side, y, core)

            @pl.when(jnp.logical_not(jnp.logical_and(native, x_lo == side)))
            def _():
                await_shard(h, index)

            forward(h, index, y_up)
            forward(h, index, y_down)
            forward(h, index, partner)

    def first_hop(h):
        for side, dy, onward in ((0, -1, y_up), (1, 1, y_down), (1, -1, None), (0, 1, None)):
            index = _seq(side, y + dy, core)
            await_shard(h, index)
            if onward is not None:
                forward(h, index, onward)
            forward(h, index, partner)

    def second_hop(h):
        for side in range(2):
            index = _seq(side, y + 2, core)
            await_shard(h, index)
            forward(h, index, partner)

    def other_core(h):
        for side in range(2):
            for dy in range(YS):
                await_shard(h, _seq(side, y + dy, core + 1))

    def attend(h, queries, allowed=None):
        scores = lax.dot_general(
            queries, kv[h, 0], (((1,), (1,)), ((), ())), preferred_element_type=jnp.float32
        )
        weights = _silu_weights(scores)
        if allowed is not None:
            weights = jnp.where(allowed, weights, 0.0)
        return jnp.dot(
            weights.astype(jnp.bfloat16), kv[h, 1], preferred_element_type=jnp.float32
        )

    def prepare():
        for t in range(TILES * TILE // ROWS):
            cand_g[pl.ds(t * ROWS, ROWS), :] = _every_second(
                cand_rows[pl.ds(t * 2 * ROWS, 2 * ROWS), :], 1
            )
        hist_g[...] = _every_second(qu_ref[0].reshape(2 * ROWS, WIDTH), 1)
        for t in range(TILES * TILE // ROWS):
            held = slot_rows(t * ROWS + lax.broadcasted_iota(jnp.int32, (ROWS, 128), 0))
            at = lax.broadcasted_iota(jnp.int32, (ROWS, PACKED), 1)
            pick[pl.ds(t * ROWS, ROWS), :] = jnp.where(at == held[:, :1], 1.0, 0.0).astype(jnp.bfloat16)

    r_copies = []

    def group(h, g):
        first, count = GROUPS[g]
        if h % QUERY_HEADS == 0:
            for m in range(max(first, 1), first + count):
                q_copies[m, h].wait_recv()
        rows = pl.ds(first * PACK, count * PACK)
        part = columns(h, 1)
        computed[rows, part] = attend(h, arrived[rows, part]).astype(jnp.bfloat16)
        if (h + 1) % BACK_HEADS:
            return
        start = h + 1 - BACK_HEADS
        for m in range(first, first + count):
            part = (pl.ds(m * PACK, PACK), columns(start, BACK_HEADS))
            if m:
                copy = _send(
                    computed.at[part],
                    returned.at[part],
                    r_send.at[m, start],
                    r_recv.at[m, start],
                    peer(m, True),
                )
                copy.start()
                r_copies.append(copy)
            else:
                returned[part] = computed[part]

    enter(0)
    enter(1)
    first_hop(0)
    prepare()
    enter(2)
    first_hop(1)
    second_hop(0)
    enter(3)
    other_core(0)
    first_hop(2)
    second_hop(1)
    first_hop(3)
    second_hop(2)
    group(0, 0)
    other_core(1)
    second_hop(3)
    group(0, 1)
    group(1, 0)
    other_core(2)
    group(1, 1)
    group(2, 0)
    other_core(3)
    group(2, 1)
    group(3, 0)
    group(3, 1)

    back_over = _send(
        hist_done.at[pl.ds(ROWS, ROWS)],
        hist_done.at[pl.ds(0, ROWS)],
        h_send.at[1],
        h_recv.at[1],
        x_other,
    )

    @pl.when(native)
    def _():
        q_over.wait_recv()
        other = _seq(x_lo + 1, y, core)
        key_at = lax.broadcasted_iota(jnp.int32, (2 * ROWS, LENGTH), 1)
        row_at = lax.broadcasted_iota(jnp.int32, (2 * ROWS, LENGTH), 0)
        row_at = row_at + jnp.where(row_at < ROWS, seq * ROWS, (other - 1) * ROWS)
        for h in range(HEADS):
            part = slice(h * HEAD_DIM, (h + 1) * HEAD_DIM)
            hist_done[:, part] = attend(h, hist_q[:, part], key_at <= row_at).astype(jnp.bfloat16)
        back_over.start()

    @pl.when(jnp.logical_not(native))
    def _():
        back_over.wait_recv()

    loads[5].wait()
    loads[6].wait()
    hist_rows = jnp.dot(
        _gate(_normalise(hist_done[:ROWS, :].astype(jnp.float32)), hist_g[...]), w_ref[...], preferred_element_type=jnp.float32
    ) + x_ref[0].astype(jnp.float32)
    row = seq * ROWS + lax.broadcasted_iota(jnp.int32, (ROWS, MODEL), 0)
    hist_out[0] = jnp.where(row < limit, hist_rows, 0.0).astype(jnp.bfloat16)

    for copy in r_copies:
        copy.wait_recv()
    picked = jnp.dot(pick[...], returned[...], preferred_element_type=jnp.float32)
    cand_out[0, 0] = jnp.dot(
        _gate(_normalise(picked), cand_g[...]), w_ref[...], preferred_element_type=jnp.float32
    ).astype(jnp.bfloat16)

    for copy in to_far:
        copy.wait_send()

    @pl.when(jnp.logical_not(native))
    def _():
        for copy in to_near:
            copy.wait_send()
        q_over.wait_send()

    @pl.when(native)
    def _():
        back_over.wait_send()

    for copy in kv_copies + list(q_copies.values()) + r_copies:
        copy.wait_send()


def local(hist_qu, hist_kv, hist_x, lengths, cand_qu, cand_owner, w_out):
    vmem = pl.BlockSpec(memory_space=pltpu.VMEM)
    hbm = pl.BlockSpec(memory_space=pltpu.HBM)
    arguments = (hist_qu, hist_kv, hist_x, lengths, cand_qu, cand_owner, w_out)
    bf16 = jnp.bfloat16
    return pl.pallas_call(
        kernel,
        out_shape=(
            jax.ShapeDtypeStruct((1, ROWS, MODEL), bf16),
            jax.ShapeDtypeStruct((1, 1, CROWS, MODEL), bf16),
        ),
        in_specs=[hbm] * len(arguments),
        out_specs=(vmem, vmem),
        scratch_shapes=[
            (pltpu.SMEM if a.dtype == jnp.int32 else pltpu.VMEM)(a.shape, a.dtype)
            for a in arguments
        ]
        + [
            pltpu.VMEM((HEADS, 2, ROWS, HEAD_DIM), bf16),
            pltpu.VMEM((HEADS, 2, LENGTH, HEAD_DIM), bf16),
            pltpu.VMEM((2 * ROWS, WIDTH), bf16),
            pltpu.VMEM((2 * ROWS, WIDTH), bf16),
            pltpu.VMEM((2 * CROWS, WIDTH), bf16),
            pltpu.VMEM((CROWS, WIDTH), bf16),
            pltpu.VMEM((ROWS, WIDTH), bf16),
            pltpu.VMEM((PACKED, WIDTH), bf16),
            pltpu.VMEM((PACKED, WIDTH), bf16),
            pltpu.VMEM((PACKED, WIDTH), bf16),
            pltpu.VMEM((PACKED, WIDTH), bf16),
            pltpu.VMEM((CROWS, PACKED), bf16),
            pltpu.SemaphoreType.DMA((len(arguments),)),
            pltpu.SemaphoreType.DMA((64,)),
            pltpu.SemaphoreType.DMA((16, HEADS)),
            pltpu.SemaphoreType.DMA((MESSAGES, HEADS)),
            pltpu.SemaphoreType.DMA((MESSAGES, HEADS)),
            pltpu.SemaphoreType.DMA((MESSAGES, HEADS)),
            pltpu.SemaphoreType.DMA((MESSAGES, HEADS)),
            pltpu.SemaphoreType.DMA((2,)),
            pltpu.SemaphoreType.DMA((2,)),
        ],
        compiler_params=pltpu.CompilerParams(
            collective_id=0, has_side_effects=True, vmem_limit_bytes=63 * 2**20
        ),
    )(*arguments)


def solution(mesh):
    placed = (
        P("users", "seq", None, None),
        P("users", "seq", None, None),
        P("users", "seq", None),
        P("users"),
        P("users", "seq", None, None, None),
        P("users", "seq", None),
        P(),
    )
    return jax.shard_map(
        local,
        mesh=mesh,
        in_specs=placed,
        out_specs=(P("users", "seq", None), P("users", "seq", None, None)),
        check_vma=False,
    )
```

time: 80.1 us -> 62.7 us (0.78)
  the two profiles are of different devices: /device:TPU:1 before, /device:TPU:32 now
where the time goes in v2:
time: 62.7 us; the launch traced here: 61.6 us
  Pallas kernels  56.6 us (90%)
  local copies, waits for them, and re-layouts  3.73 us (6%)
  between operations  1.29 us (2%)
    pallas_call x1, Pallas kernels, local(): pl.pallas_call(kernel, out_shape=(jax.ShapeDtypeStruct((1, ROWS, MODEL),...  56.6 us
    unnamed x2, local copies, waits for them, and re-layouts  3.73 us

profile of v2, /device:TPU:32, one launch (start us, length us, event | category | flops | bytes accessed | tf_op | source)
XLA Modules:
  0.0 61.6 jit_solution(14954250827595313062)
XLA Ops:
  1.3 56.6 %shard_map.86 = (bf16[1,128,1024]{2,1,0:T(8,128)(2,1)}, bf16[1,1,384,1024]{3,2,1,0:T(8,128)(2,1)}) custom-call(bf16[1,128,2,512]{3,2,1,0:T(2,128)(2,1)} %qu_hbm.1, bf16[1,128,2,512]{3,2,1,0:T(2,128)(2,1)} %kv_hbm.1, bf16[1,128,1024]{2,1,0:T(8,128)(2,1)} %x_hbm.1, s32[1]{0:T(128)S(6)} %copy.11.lengths_hbm, bf16[1,1,384,2,512]{4,3,2,1,0:T(2,128)(2,1)} %cand_hbm.1, ...), custom_call_target="tpu_custom_call" | custom-call | tf_op jit(solution)/shard_map/pallas_call | solution.py:414
  57.9 1.7 %copy.12 = bf16[1,128,1024]{2,1,0:T(8,128)(2,1)} copy(bf16[1,128,1024]{2,1,0:T(8,128)(2,1)} %get-tuple-element.4) | data formatting | bytes 524288
  59.6 2.1 %copy.13 = bf16[1,1,384,1024]{3,2,1,0:T(8,128)(2,1)} copy(bf16[1,1,384,1024]{3,2,1,0:T(8,128)(2,1)} %get-tuple-element.5) | data formatting | bytes 1572864

commit v3 on v2

--- a/solution.py
+++ b/solution.py
@@ -28,6 +28,7 @@
 PACK = CAP * TILE
 PACKED = MESSAGES * PACK
 GROUPS = ((0, 8), (8, 8))
+AHEAD = 2
 QUERY_HEADS = 1
 BACK_HEADS = 1
 
@@ -161,14 +162,19 @@
     q_over = _send(
         hist_q.at[pl.ds(0, ROWS)], hist_q.at[pl.ds(ROWS, ROWS)], h_send.at[0], h_recv.at[0], x_other
     )
-    for copy in to_far:
-        copy.start()
-
-    @pl.when(jnp.logical_not(native))
-    def _():
-        for copy in to_near:
-            copy.start()
-        q_over.start()
+    def own_shard(h):
+        if h >= 2:
+            to_far[h - 2].wait_send()
+        to_far[h].start()
+
+        @pl.when(jnp.logical_not(native))
+        def _():
+            if h >= 2:
+                to_near[h - 2].wait_send()
+            to_near[h].start()
+
+    own_shard(0)
+    own_shard(1)
 
     @pl.when(native)
     def _():
@@ -217,7 +223,8 @@
         return pl.ds(first * HEAD_DIM, count * HEAD_DIM)
 
     q_copies = {}
-    for h in range(0, HEADS, QUERY_HEADS):
+
+    def send_queries(h):
         for m in Q_ORDER:
             part = (pl.ds(m * PACK, PACK), columns(h, QUERY_HEADS))
             q_copies[m, h] = _send(
@@ -225,7 +232,7 @@
             )
             q_copies[m, h].start()
 
-    kv_copies = []
+    kv_copies, kv_settled = [], []
 
     def forward(h, index, device):
         copy = _send(
@@ -237,13 +244,21 @@
         )
         copy.start()
         kv_copies.append(copy)
+        return copy
 
     def await_shard(h, index):
         _send(
             shard(h, index), shard(h, index), kv_send.at[0], kv_recv.at[index, h], partner
         ).wait_recv()
 
+    entries = []
+
     def enter(h):
+        if h >= AHEAD:
+            for copy in entries[h - AHEAD]:
+                copy.wait_send()
+                kv_settled.append(copy)
+        entries.append([])
         for side in range(2):
             index = _seq(side, y, core)
 
@@ -251,8 +266,8 @@
             def _():
                 await_shard(h, index)
 
-            forward(h, index, y_up)
-            forward(h, index, y_down)
+            entries[h].append(forward(h, index, y_up))
+            entries[h].append(forward(h, index, y_down))
             forward(h, index, partner)
 
     def first_hop(h):
@@ -324,29 +339,40 @@
             else:
                 returned[part] = computed[part]
 
+    own_shard(2)
     enter(0)
+    own_shard(3)
+    send_queries(0)
+
+    @pl.when(jnp.logical_not(native))
+    def _():
+        q_over.start()
+
     enter(1)
     first_hop(0)
-    prepare()
     enter(2)
+    send_queries(1)
     first_hop(1)
     second_hop(0)
     enter(3)
+    send_queries(2)
+    send_queries(3)
+    prepare()
     other_core(0)
     first_hop(2)
     second_hop(1)
+    group(0, 0)
     first_hop(3)
     second_hop(2)
-    group(0, 0)
+    group(0, 1)
     other_core(1)
+    group(1, 0)
     second_hop(3)
-    group(0, 1)
-    group(1, 0)
+    group(1, 1)
     other_core(2)
-    group(1, 1)
     group(2, 0)
+    group(2, 1)
     other_core(3)
-    group(2, 1)
     group(3, 0)
     group(3, 1)
 
@@ -389,21 +415,22 @@
         _gate(_normalise(picked), cand_g[...]), w_ref[...], preferred_element_type=jnp.float32
     ).astype(jnp.bfloat16)
 
-    for copy in to_far:
-        copy.wait_send()
+    for h in (2, 3):
+        to_far[h].wait_send()
 
     @pl.when(jnp.logical_not(native))
     def _():
-        for copy in to_near:
+        for h in (2, 3):
+            to_near[h].wait_send()
+        q_over.wait_send()
+
+    @pl.when(native)
+    def _():
+        back_over.wait_send()
+
+    for copy in kv_copies + list(q_copies.values()) + r_copies:
+        if not any(copy is done for done in kv_settled):
             copy.wait_send()
-        q_over.wait_send()
-
-    @pl.when(native)
-    def _():
-        back_over.wait_send()
-
-    for copy in kv_copies + list(q_copies.values()) + r_copies:
-        copy.wait_send()
 
 
 def local(hist_qu, hist_kv, hist_x, lengths, cand_qu, cand_owner, w_out):

time: 62.7 us -> 61.1 us (0.974)
  Pallas kernels: 56.6 us -> 55.4 us
    pallas_call x1, Pallas kernels: 56.6 us -> 55.4 us  [local(): pl.pallas_call(kernel, out_shape=(jax.ShapeDtypeStruct((1, ROWS, MODEL),...]
where the time goes in v3:
time: 61.1 us; the launch traced here: 60.5 us
  Pallas kernels  55.4 us (91%)
  local copies, waits for them, and re-layouts  3.73 us (6%)
  between operations  1.29 us (2%)
    pallas_call x1, Pallas kernels, local(): pl.pallas_call(kernel, out_shape=(jax.ShapeDtypeStruct((1, ROWS, MODEL),...  55.4 us
    unnamed x2, local copies, waits for them, and re-layouts  3.73 us

profile of v3, /device:TPU:32, one launch (start us, length us, event | category | flops | bytes accessed | tf_op | source)
XLA Modules:
  0.0 60.5 jit_solution(13022147694002764773)
XLA Ops:
  1.3 55.4 %shard_map.86 = (bf16[1,128,1024]{2,1,0:T(8,128)(2,1)}, bf16[1,1,384,1024]{3,2,1,0:T(8,128)(2,1)}) custom-call(bf16[1,128,2,512]{3,2,1,0:T(2,128)(2,1)} %qu_hbm.1, bf16[1,128,2,512]{3,2,1,0:T(2,128)(2,1)} %kv_hbm.1, bf16[1,128,1024]{2,1,0:T(8,128)(2,1)} %x_hbm.1, s32[1]{0:T(128)S(6)} %copy.11.lengths_hbm, bf16[1,1,384,2,512]{4,3,2,1,0:T(2,128)(2,1)} %cand_hbm.1, ...), custom_call_target="tpu_custom_call" | custom-call | tf_op jit(solution)/shard_map/pallas_call | solution.py:441
  56.7 1.7 %copy.12 = bf16[1,128,1024]{2,1,0:T(8,128)(2,1)} copy(bf16[1,128,1024]{2,1,0:T(8,128)(2,1)} %get-tuple-element.4) | data formatting | bytes 524288
  58.4 2.1 %copy.13 = bf16[1,1,384,1024]{3,2,1,0:T(8,128)(2,1)} copy(bf16[1,1,384,1024]{3,2,1,0:T(8,128)(2,1)} %get-tuple-element.5) | data formatting | bytes 1572864

commit v4 on v3

--- a/solution.py
+++ b/solution.py
@@ -28,7 +28,7 @@
 PACK = CAP * TILE
 PACKED = MESSAGES * PACK
 GROUPS = ((0, 8), (8, 8))
-AHEAD = 2
+AHEAD = 4
 QUERY_HEADS = 1
 BACK_HEADS = 1
 
@@ -324,7 +324,7 @@
         if (h + 1) % BACK_HEADS:
             return
         start = h + 1 - BACK_HEADS
-        for m in range(first, first + count):
+        for m in reversed(range(first, first + count)):
             part = (pl.ds(m * PACK, PACK), columns(start, BACK_HEADS))
             if m:
                 copy = _send(
@@ -340,31 +340,29 @@
                 returned[part] = computed[part]
 
     own_shard(2)
+    send_queries(0)
     enter(0)
     own_shard(3)
-    send_queries(0)
-
+    send_queries(1)
     @pl.when(jnp.logical_not(native))
     def _():
         q_over.start()
-
     enter(1)
     first_hop(0)
+    send_queries(2)
     enter(2)
-    send_queries(1)
+    send_queries(3)
     first_hop(1)
     second_hop(0)
     enter(3)
-    send_queries(2)
-    send_queries(3)
     prepare()
     other_core(0)
     first_hop(2)
+    group(0, 0)
     second_hop(1)
-    group(0, 0)
     first_hop(3)
+    group(0, 1)
     second_hop(2)
-    group(0, 1)
     other_core(1)
     group(1, 0)
     second_hop(3)
@@ -373,8 +371,8 @@
     group(2, 0)
     group(2, 1)
     other_core(3)
+    group(3, 1)
     group(3, 0)
-    group(3, 1)
 
     back_over = _send(
         hist_done.at[pl.ds(ROWS, ROWS)],

time: 61.1 us -> 59.8 us (0.979)
  Pallas kernels: 55.4 us -> 54.6 us
    pallas_call x1, Pallas kernels: 55.4 us -> 54.6 us  [local(): pl.pallas_call(kernel, out_shape=(jax.ShapeDtypeStruct((1, ROWS, MODEL),...]
where the time goes in v4:
time: 59.8 us; the launch traced here: 59.7 us
  Pallas kernels  54.6 us (91%)
  local copies, waits for them, and re-layouts  3.73 us (6%)
  between operations  1.29 us (2%)
    pallas_call x1, Pallas kernels, local(): pl.pallas_call(kernel, out_shape=(jax.ShapeDtypeStruct((1, ROWS, MODEL),...  54.6 us
    unnamed x2, local copies, waits for them, and re-layouts  3.73 us

profile of v4, /device:TPU:32, one launch (start us, length us, event | category | flops | bytes accessed | tf_op | source)
XLA Modules:
  0.0 59.7 jit_solution(6498602292323237599)
XLA Ops:
  1.3 54.6 %shard_map.86 = (bf16[1,128,1024]{2,1,0:T(8,128)(2,1)}, bf16[1,1,384,1024]{3,2,1,0:T(8,128)(2,1)}) custom-call(bf16[1,128,2,512]{3,2,1,0:T(2,128)(2,1)} %qu_hbm.1, bf16[1,128,2,512]{3,2,1,0:T(2,128)(2,1)} %kv_hbm.1, bf16[1,128,1024]{2,1,0:T(8,128)(2,1)} %x_hbm.1, s32[1]{0:T(128)S(6)} %copy.11.lengths_hbm, bf16[1,1,384,2,512]{4,3,2,1,0:T(2,128)(2,1)} %cand_hbm.1, ...), custom_call_target="tpu_custom_call" | custom-call | tf_op jit(solution)/shard_map/pallas_call | solution.py:439
  55.9 1.7 %copy.12 = bf16[1,128,1024]{2,1,0:T(8,128)(2,1)} copy(bf16[1,128,1024]{2,1,0:T(8,128)(2,1)} %get-tuple-element.4) | data formatting | bytes 524288
  57.6 2.1 %copy.13 = bf16[1,1,384,1024]{3,2,1,0:T(8,128)(2,1)} copy(bf16[1,1,384,1024]{3,2,1,0:T(8,128)(2,1)} %get-tuple-element.5) | data formatting | bytes 1572864
